TPU v7x, 32 devices: a whole 2x2x4 slice. The times are simulated.
32 devices in a mesh: blk: 16 (over z, y, core), uly: 2 (over x).
Axes of the slice: x: 2, y: 2, z: 4, core: 2. Of those that a mesh axis runs over, the one named last changes fastest.
Arguments:
- query: bfloat16 [4096, 3072], P(('blk', 'uly')), may hold values from -40 to 40
- keys: bfloat16 [4096, 3072], P(('blk', 'uly')), may hold values from -5.2 to 5.2
- values: bfloat16 [4096, 3072], P(('blk', 'uly')), may hold values from -5 to 5
- block_mask: int32 [32, 32], P('blk'), may hold values from 0 to 1, as said below
Outputs:
- grad_query: bfloat16 [4096, 3072], P(('blk', 'uly'))
- grad_keys: bfloat16 [4096, 3072], P(('blk', 'uly'))
- grad_values: bfloat16 [4096, 3072], P(('blk', 'uly'))
Inputs may be any that keep to these rules, and one draw needn't show every extreme that they name: block_mask is symmetric, its diagonal is all ones, it is zero wherever |i - j| > 2, and each row holds at most 5 ones, some rows exactly 5.
All inputs are finite; a program needn't handle non-finite values.
Results may differ from a plain program's by a relative error of at most 0.017.
Values may be sent and summed in bfloat16 or wider, within the bound.
A program may use at most 128 MiB of HBM per device.

v0:
```python
import jax
import jax.numpy as jnp
from jax import lax
from jax.sharding import PartitionSpec as P

HD = 128
BLK = 128
M = 5


loss_scale = 64.0
masked = -1e30


def padded(cells, sides, width):
    for axis, dim in sides:
        count = lax.axis_size(axis)
        ends = count - 1
        head = lax.slice_in_dim(cells, 0, width, axis=dim)
        tail = lax.slice_in_dim(cells, cells.shape[dim] - width, cells.shape[dim], axis=dim)
        cells = jnp.concatenate(
            [
                lax.ppermute(tail, axis, [(i, (i + 1) % count) for i in range(ends)]),
                cells,
                lax.ppermute(head, axis, [((i + 1) % count, i) for i in range(ends)]),
            ],
            axis=dim,
        )
    return cells


def from_behind(value, axis, steps):
    count = lax.axis_size(axis)
    initial, last = (max(0, -steps), min(count, count - steps))
    return lax.ppermute(value, axis, [(source, source + steps) for source in range(initial, last)])


def block_lists(rows, count):
    width = rows.shape[-1]
    running = jnp.cumsum(rows, axis=-1)
    ranks = jnp.arange(1, count + 1, dtype=jnp.int32)
    hits = (rows[..., None, :] == 1) & (running[..., None, :] == ranks[:, None])
    columns = jnp.arange(width, dtype=jnp.int32)
    slot_index = jnp.sum(jnp.where(hits, columns, 0), axis=-1)
    slot_valid = jnp.any(hits, axis=-1)
    return (slot_index, slot_valid)


def attend_rows(query_one, key_window, value_window, slot_index, slot_valid, scale):
    key_tiles = key_window[slot_index]
    value_tiles = value_window[slot_index]
    scores = (
        jnp.einsum("rtd,rmud->rtmu", query_one, key_tiles, preferred_element_type=jnp.float32)
        * scale
    )
    scores = jnp.where(slot_valid[:, None, :, None], scores, masked)
    row_top = jnp.max(scores, axis=(2, 3))
    log_total = row_top + jnp.log(jnp.sum(jnp.exp(scores - row_top[:, :, None, None]), axis=(2, 3)))
    weights = jnp.exp(scores - log_total[:, :, None, None])
    weights_b = weights.astype(jnp.bfloat16)
    attended = jnp.einsum(
        "rtmu,rmud->rtd", weights_b, value_tiles, preferred_element_type=jnp.float32
    )
    grad_out = (loss_scale * attended).astype(jnp.bfloat16)
    row_delta = jnp.sum(grad_out.astype(jnp.float32) * attended, axis=2)
    grad_weights = jnp.einsum(
        "rtd,rmud->rtmu", grad_out, value_tiles, preferred_element_type=jnp.float32
    )
    grad_scores = weights * (grad_weights - row_delta[:, :, None, None])
    grad_scores_b = grad_scores.astype(jnp.bfloat16)
    grad_one = (
        jnp.einsum("rtmu,rmud->rtd", grad_scores_b, key_tiles, preferred_element_type=jnp.float32)
        * scale
    ).astype(jnp.bfloat16)
    return (grad_one, grad_out, log_total, row_delta, weights_b, grad_scores_b)


def heads_first(array, heads_all):
    return jnp.transpose(array.reshape(array.shape[0], heads_all, HD), (1, 0, 2))


def tokens_first(array):
    return jnp.transpose(array, (1, 0, 2)).reshape(array.shape[1], array.shape[0] * HD)


def body(query, keys, values, block_mask):
    scale = HD ** (-0.5)
    heads_all = query.shape[1] // HD
    query_heads, key_heads, value_heads = (
        lax.all_to_all(
            heads_first(query, heads_all), "uly", split_axis=0, concat_axis=1, tiled=True
        ),
        lax.all_to_all(
            heads_first(keys, heads_all), "uly", split_axis=0, concat_axis=1, tiled=True
        ),
        lax.all_to_all(
            heads_first(values, heads_all), "uly", split_axis=0, concat_axis=1, tiled=True
        ),
    )
    heads_here = query_heads.shape[0]
    group_tokens = query_heads.shape[1]
    group_blocks = group_tokens // BLK
    position = lax.axis_index("blk")
    padded_mask = jnp.pad(block_mask, ((0, 0), (group_blocks, group_blocks)))
    window_mask = lax.dynamic_slice_in_dim(
        padded_mask, position * group_blocks, 3 * group_blocks, 1
    )
    slot_index, slot_valid = block_lists(window_mask, M)
    key_value = jnp.stack([key_heads, value_heads])
    beside_all = padded(key_value, (("blk", 2),), group_tokens)
    key_window = beside_all[0].reshape(heads_here, 3 * group_blocks, BLK, HD)
    value_window = beside_all[1].reshape(heads_here, 3 * group_blocks, BLK, HD)
    query_blocks = query_heads.reshape(heads_here, group_blocks, BLK, HD)

    def per_head(items):
        query_one, key_win, value_win = items
        grad_one, grad_out, log_total, row_delta, weights_b, grad_scores_b = attend_rows(
            query_one, key_win, value_win, slot_index, slot_valid, scale
        )
        value_part = jnp.einsum(
            "rtmu,rtd->rmud", weights_b, grad_out, preferred_element_type=jnp.float32
        )
        key_part = (
            jnp.einsum(
                "rtmu,rtd->rmud", grad_scores_b, query_one, preferred_element_type=jnp.float32
            )
            * scale
        )
        flat_index = slot_index.reshape(-1)
        empty_slots = jnp.zeros((3 * group_blocks, BLK, HD), jnp.float32)
        key_slots = empty_slots.at[flat_index].add(key_part.reshape(-1, BLK, HD))
        value_slots = empty_slots.at[flat_index].add(value_part.reshape(-1, BLK, HD))
        return (grad_one, key_slots, value_slots)

    grad_blocks, key_slots, value_slots = lax.map(
        per_head, (query_blocks, key_window, value_window)
    )
    slot_sums = jnp.stack([key_slots, value_slots]).reshape(2, heads_here, 3 * group_tokens, HD)
    from_upper = from_behind(slot_sums[:, :, :group_tokens].astype(jnp.bfloat16), "blk", -1).astype(
        jnp.float32
    )
    from_lower = from_behind(
        slot_sums[:, :, 2 * group_tokens :].astype(jnp.bfloat16), "blk", 1
    ).astype(jnp.float32)
    totals = slot_sums[:, :, group_tokens : 2 * group_tokens] + from_upper + from_lower
    grad_key_heads = totals[0].astype(jnp.bfloat16)
    grad_value_heads = totals[1].astype(jnp.bfloat16)
    grad_query_heads = grad_blocks.reshape(heads_here, group_tokens, HD)
    back_query, back_keys, back_values = (
        lax.all_to_all(grad_query_heads, "uly", split_axis=1, concat_axis=0, tiled=True),
        lax.all_to_all(grad_key_heads, "uly", split_axis=1, concat_axis=0, tiled=True),
        lax.all_to_all(grad_value_heads, "uly", split_axis=1, concat_axis=0, tiled=True),
    )
    return (tokens_first(back_query), tokens_first(back_keys), tokens_first(back_values))


def solution(mesh):
    in_specs = (
        P(("blk", "uly"), None),
        P(("blk", "uly"), None),
        P(("blk", "uly"), None),
        P("blk", None),
    )
    out_specs = (P(("blk", "uly"), None), P(("blk", "uly"), None), P(("blk", "uly"), None))
    return jax.shard_map(body, mesh=mesh, in_specs=in_specs, out_specs=out_specs, check_vma=False)
```

profile of v0, /device:TPU:9, one launch (start us, length us, event | category | flops | bytes accessed | tf_op | source)
XLA Modules:
  0.0 271.6 jit_solution(15878410714864742777)
XLA Ops:
  0.6 2.3 copy.118
  2.9 3.5 %all-to-all-start.1 = ((bf16[24,128,128]{1,2,0:T(8,128)(2,1)}), bf16[24,128,128]{1,2,0:T(8,128)(2,1)S(1)}, u32[]{:S(2)}, u32[]{:S(2)}) async-start(bf16[24,128,128]{1,2,0:T(8,128)(2,1)} %bitcast.27), calls=%async_computation.1 | async-start | bytes 1572864 | tf_op jit(solution)/shard_map/all_to_all | solution.py:93
  6.5 2.3 copy.121
  8.7 7.9 %all-to-all-done.1 = bf16[24,128,128]{1,2,0:T(8,128)(2,1)S(1)} async-done(((bf16[24,128,128]{1,2,0:T(8,128)(2,1)}), bf16[24,128,128]{1,2,0:T(8,128)(2,1)S(1)}, u32[]{:S(2)}, u32[]{:S(2)}) %all-to-all-start.1) | async-done | bytes 786464 | tf_op jit(solution)/shard_map/all_to_all | solution.py:93
  16.6 3.5 %all-to-all-start.2 = ((bf16[24,128,128]{1,2,0:T(8,128)(2,1)}), bf16[24,128,128]{1,2,0:T(8,128)(2,1)S(1)}, u32[]{:S(2)}, u32[]{:S(2)}) async-start(bf16[24,128,128]{1,2,0:T(8,128)(2,1)} %bitcast.33), calls=%async_computation.2 | async-start | bytes 1572864 | tf_op jit(solution)/shard_map/all_to_all | solution.py:96
  20.6 8.9 %all-to-all-done.2 = bf16[24,128,128]{1,2,0:T(8,128)(2,1)S(1)} async-done(((bf16[24,128,128]{1,2,0:T(8,128)(2,1)}), bf16[24,128,128]{1,2,0:T(8,128)(2,1)S(1)}, u32[]{:S(2)}, u32[]{:S(2)}) %all-to-all-start.2) | async-done | bytes 786464 | tf_op jit(solution)/shard_map/all_to_all | solution.py:96
  31.1 4.4 %collective-permute-start.1 = (bf16[2,12,256,128]{3,2,1,0:T(8,128)(2,1)}, bf16[2,12,256,128]{3,2,1,0:T(8,128)(2,1)}, u32[]{:S(2)}, u32[]{:S(2)}) collective-permute-start(bf16[2,12,256,128]{3,2,1,0:T(8,128)(2,1)} %pad_maximum_fusion.2), channel_id=1, source_target_pairs={{2,0},{4,2},{6,4},{8,6},{10,8},{12,10},{14,12},{16,14},{18,16},{20... | collective-permute-start | bytes 4718600 | tf_op jit(solution)/shard_map/ppermute | solution.py:25
  35.5 3.0 %collective-permute-start = (bf16[2,12,256,128]{3,2,1,0:T(8,128)(2,1)}, bf16[2,12,256,128]{3,2,1,0:T(8,128)(2,1)}, u32[]{:S(2)}, u32[]{:S(2)}) collective-permute-start(bf16[2,12,256,128]{3,2,1,0:T(8,128)(2,1)} %pad_maximum_fusion.2), channel_id=1, source_target_pairs={{0,2},{2,4},{4,6},{6,8},{8,10},{10,12},{12,14},{14,16},{16,18},{18... | collective-permute-start | bytes 4718600 | tf_op jit(solution)/shard_map/ppermute | solution.py:23
  38.6 2.3 copy.116
  40.9 3.5 %all-to-all-start = ((bf16[24,128,128]{1,2,0:T(8,128)(2,1)}), bf16[24,128,128]{1,2,0:T(8,128)(2,1)S(1)}, u32[]{:S(2)}, u32[]{:S(2)}) async-start(bf16[24,128,128]{1,2,0:T(8,128)(2,1)} %bitcast.22), calls=%async_computation | async-start | bytes 1572864 | tf_op jit(solution)/shard_map/all_to_all | solution.py:90
  45.5 26.4 %collective-permute-done.1 = bf16[2,12,256,128]{3,2,1,0:T(8,128)(2,1)} collective-permute-done((bf16[2,12,256,128]{3,2,1,0:T(8,128)(2,1)}, bf16[2,12,256,128]{3,2,1,0:T(8,128)(2,1)}, u32[]{:S(2)}, u32[]{:S(2)}) %collective-permute-start.1) | collective-permute-done | bytes 1572896 | tf_op jit(solution)/shard_map/ppermute | solution.py:25
  74.0 2.5 fusion.33
  76.6 114.6 %while.15 = (s32[]{:T(128)}, bf16[12,2,128,128]{3,2,1,0:T(8,128)(2,1)}, f32[12,6,128,128]{3,2,1,0:T(8,128)}, f32[12,6,128,128]{3,2,1,0:T(8,128)}, pred[2,5]{1,0:...) while((s32[]{:T(128)}, ...), condition=%wide.wide.region_9.10_spmd, body=%wide.wide.region_3.9_spmd.sunk | while | flops 254640704 | bytes 15876181 | solution.py:135
  191.2 4.5 %fusion.23 = bf16[2,12,768,128]{3,2,1,0:T(8,128)(2,1)S(1)} fusion(f32[1,12,768,128]{3,2,1,0:T(8,128)} %bitcast.183, f32[1,12,768,128]{3,2,1,0:T(8,128)} %bitcast.185), kind=kLoop, calls=%fused_computation.43 | loop fusion | flops 2359296 | bytes 14155776 | tf_op jit(solution)/shard_map/convert.3
  199.6 3.7 %collective-permute-start.3 = (bf16[2,12,256,128]{3,2,1,0:T(8,128)(2,1)}, bf16[2,12,256,128]{3,2,1,0:T(8,128)(2,1)}, u32[]{:S(2)}, u32[]{:S(2)}) collective-permute-start(bf16[2,12,256,128]{3,2,1,0:T(8,128)(2,1)} %get-tuple-element.139), channel_id=1, source_target_pairs={{0,2},{2,4},{4,6},{6,8},{8,10},{10,12},{12,14},{14,16},{16,18},{18... | collective-permute-start | bytes 4718600 | tf_op jit(solution)/shard_map/ppermute | solution.py:35
  203.3 2.7 copy.126
  206.0 3.6 %all-to-all-start.3 = ((bf16[12,256,128]{2,0,1:T(8,128)(2,1)}), bf16[12,256,128]{2,0,1:T(8,128)(2,1)S(1)}, u32[]{:S(2)}, u32[]{:S(2)}) async-start(bf16[12,256,128]{2,0,1:T(8,128)(2,1)} %bitcast.40), calls=%async_computation.3 | async-start | bytes 2097152 | tf_op jit(solution)/shard_map/all_to_all | solution.py:150
  209.6 27.3 %collective-permute-done.2 = bf16[2,12,256,128]{3,2,1,0:T(8,128)(2,1)S(1)} collective-permute-done((bf16[2,12,256,128]{3,2,1,0:T(8,128)(2,1)}, bf16[2,12,256,128]{3,2,1,0:T(8,128)(2,1)S(1)}, u32[]{:S(2)}, u32[]{:S(2)}) %collective-permute-start.2) | collective-permute-done | bytes 1572896 | tf_op jit(solution)/shard_map/ppermute | solution.py:35
  236.9 3.0 %fusion.27 = bf16[2,12,256,128]{3,2,1,0:T(8,128)(2,1)S(1)} fusion(f32[1,12,768,128]{3,2,1,0:T(8,128)} %bitcast.186, f32[1,12,768,128]{3,2,1,0:T(8,128)} %bitcast.184, bf16[2,12,256,128]{3,2,1,0:T(8,128)(2,1)} %collective-permute-done.3, bf16[2,12,256,128]{3,2,1,0:T(8,128)(2,1)S(1)} %collective-permute-done.2), kind=kLoop, calls=%fused_computation.48 | loop fusion | flops 4718592 | bytes 14155776 | tf_op jit(solution)/shard_map/convert.1
  241.5 3.6 %all-to-all-start.5 = ((bf16[12,256,128]{2,0,1:T(8,128)(2,1)}), bf16[12,256,128]{2,0,1:T(8,128)(2,1)S(1)}, u32[]{:S(2)}, u32[]{:S(2)}) async-start(bf16[12,256,128]{2,0,1:T(8,128)(2,1)} %copy.134), calls=%async_computation.5 | async-start | bytes 2097152 | tf_op jit(solution)/shard_map/all_to_all | solution.py:152
  246.6 11.2 %all-to-all-done.5 = bf16[12,256,128]{2,0,1:T(8,128)(2,1)S(1)} async-done(((bf16[12,256,128]{2,0,1:T(8,128)(2,1)}), bf16[12,256,128]{2,0,1:T(8,128)(2,1)S(1)}, u32[]{:S(2)}, u32[]{:S(2)}) %all-to-all-start.5) | async-done | bytes 786464 | tf_op jit(solution)/shard_map/all_to_all | solution.py:152
  257.8 3.6 %all-to-all-start.4 = ((bf16[12,256,128]{2,0,1:T(8,128)(2,1)}), bf16[12,256,128]{2,0,1:T(8,128)(2,1)S(1)}, u32[]{:S(2)}, u32[]{:S(2)}) async-start(bf16[12,256,128]{2,0,1:T(8,128)(2,1)} %copy.130), calls=%async_computation.4 | async-start | bytes 2097152 | tf_op jit(solution)/shard_map/all_to_all | solution.py:151
  262.9 2.3 copy.138
  267.2 2.4 all-to-all-done.4
  (283 shorter events, 131.3 us)
Async XLA Ops:
  2.9 13.7 %all-to-all-start.1 = ((bf16[24,128,128]{1,2,0:T(8,128)(2,1)}), bf16[24,128,128]{1,2,0:T(8,128)(2,1)S(1)}, u32[]{:S(2)}, u32[]{:S(2)}) async-start(bf16[24,128,128]{1,2,0:T(8,128)(2,1)} %bitcast.27), calls=%async_computation.1 | async-start | bytes 1572864 | tf_op jit(solution)/shard_map/all_to_all | solution.py:93
  16.6 12.8 %all-to-all-start.2 = ((bf16[24,128,128]{1,2,0:T(8,128)(2,1)}), bf16[24,128,128]{1,2,0:T(8,128)(2,1)S(1)}, u32[]{:S(2)}, u32[]{:S(2)}) async-start(bf16[24,128,128]{1,2,0:T(8,128)(2,1)} %bitcast.33), calls=%async_computation.2 | async-start | bytes 1572864 | tf_op jit(solution)/shard_map/all_to_all | solution.py:96
  20.2 24.3 %copy-start = (s32[2,32]{1,0:T(2,128)S(1)}, s32[2,32]{1,0:T(2,128)}, u32[]{:S(2)}) copy-start(s32[2,32]{1,0:T(2,128)} %param.9) | copy-start | bytes 772
  31.1 40.8 %collective-permute-start.1 = (bf16[2,12,256,128]{3,2,1,0:T(8,128)(2,1)}, bf16[2,12,256,128]{3,2,1,0:T(8,128)(2,1)}, u32[]{:S(2)}, u32[]{:S(2)}) collective-permute-start(bf16[2,12,256,128]{3,2,1,0:T(8,128)(2,1)} %pad_maximum_fusion.2), channel_id=1, source_target_pairs={{2,0},{4,2},{6,4},{8,6},{10,8},{12,10},{14,12},{16,14},{18,16},{20... | collective-permute-start | bytes 4718600 | tf_op jit(solution)/shard_map/ppermute | solution.py:25
  35.5 36.4 %collective-permute-start = (bf16[2,12,256,128]{3,2,1,0:T(8,128)(2,1)}, bf16[2,12,256,128]{3,2,1,0:T(8,128)(2,1)}, u32[]{:S(2)}, u32[]{:S(2)}) collective-permute-start(bf16[2,12,256,128]{3,2,1,0:T(8,128)(2,1)} %pad_maximum_fusion.2), channel_id=1, source_target_pairs={{0,2},{2,4},{4,6},{6,8},{8,10},{10,12},{12,14},{14,16},{16,18},{18... | collective-permute-start | bytes 4718600 | tf_op jit(solution)/shard_map/ppermute | solution.py:23
  40.9 35.7 %all-to-all-start = ((bf16[24,128,128]{1,2,0:T(8,128)(2,1)}), bf16[24,128,128]{1,2,0:T(8,128)(2,1)S(1)}, u32[]{:S(2)}, u32[]{:S(2)}) async-start(bf16[24,128,128]{1,2,0:T(8,128)(2,1)} %bitcast.22), calls=%async_computation | async-start | bytes 1572864 | tf_op jit(solution)/shard_map/all_to_all | solution.py:90
  197.7 39.2 %collective-permute-start.2 = (bf16[2,12,256,128]{3,2,1,0:T(8,128)(2,1)}, bf16[2,12,256,128]{3,2,1,0:T(8,128)(2,1)S(1)}, u32[]{:S(2)}, u32[]{:S(2)}) collective-permute-start(bf16[2,12,256,128]{3,2,1,0:T(8,128)(2,1)} %get-tuple-element.138), channel_id=1, source_target_pairs={{2,0},{4,2},{6,4},{8,6},{10,8},{12,10},{14,12},{16,14},{18,16},{20... | collective-permute-start | bytes 4718600 | tf_op jit(solution)/shard_map/ppermute | solution.py:35
  199.6 37.2 %collective-permute-start.3 = (bf16[2,12,256,128]{3,2,1,0:T(8,128)(2,1)}, bf16[2,12,256,128]{3,2,1,0:T(8,128)(2,1)}, u32[]{:S(2)}, u32[]{:S(2)}) collective-permute-start(bf16[2,12,256,128]{3,2,1,0:T(8,128)(2,1)} %get-tuple-element.139), channel_id=1, source_target_pairs={{0,2},{2,4},{4,6},{6,8},{8,10},{10,12},{12,14},{14,16},{16,18},{18... | collective-permute-start | bytes 4718600 | tf_op jit(solution)/shard_map/ppermute | solution.py:35
  206.0 35.5 %all-to-all-start.3 = ((bf16[12,256,128]{2,0,1:T(8,128)(2,1)}), bf16[12,256,128]{2,0,1:T(8,128)(2,1)S(1)}, u32[]{:S(2)}, u32[]{:S(2)}) async-start(bf16[12,256,128]{2,0,1:T(8,128)(2,1)} %bitcast.40), calls=%async_computation.3 | async-start | bytes 2097152 | tf_op jit(solution)/shard_map/all_to_all | solution.py:150
  241.5 16.3 %all-to-all-start.5 = ((bf16[12,256,128]{2,0,1:T(8,128)(2,1)}), bf16[12,256,128]{2,0,1:T(8,128)(2,1)S(1)}, u32[]{:S(2)}, u32[]{:S(2)}) async-start(bf16[12,256,128]{2,0,1:T(8,128)(2,1)} %copy.134), calls=%async_computation.5 | async-start | bytes 2097152 | tf_op jit(solution)/shard_map/all_to_all | solution.py:152
  257.8 11.8 %all-to-all-start.4 = ((bf16[12,256,128]{2,0,1:T(8,128)(2,1)}), bf16[12,256,128]{2,0,1:T(8,128)(2,1)S(1)}, u32[]{:S(2)}, u32[]{:S(2)}) async-start(bf16[12,256,128]{2,0,1:T(8,128)(2,1)} %copy.130), calls=%async_computation.4 | async-start | bytes 2097152 | tf_op jit(solution)/shard_map/all_to_all | solution.py:151
where the time goes:
time: 273 us; the launch traced here: 272 us
  waiting for transfers between devices  84 us (31%)
  local copies, waits for them, and re-layouts  76.4 us (28%)
  other arithmetic  47.6 us (17%)
  starting transfers between devices  34.4 us (13%)
  matrix products  27.2 us (10%)
    ppermute x2, waiting for transfers between devices, from_behind(): lax.ppermute(value, axis, [(source, source + steps) for source in range(i...  27.3 us
    ppermute x1, waiting for transfers between devices, padded(): lax.ppermute(head, axis, [((i + 1) % count, i) for i in range(ends)])  26.4 us
    squeeze x24, local copies, waits for them, and re-layouts, body(): lax.map(per_head, (query_blocks, key_window, value_window))  22.6 us
    scatter-add x12, other arithmetic, per_head(): empty_slots.at[flat_index].add(value_part.reshape(-1, BLK, HD))  17.2 us
    scatter-add x12, other arithmetic, per_head(): key_slots = empty_slots.at[flat_index].add(key_part.reshape(-1, BLK, HD))  17.2 us
    unnamed x9, local copies, waits for them, and re-layouts  11.6 us
    dynamic_update_slice x12, local copies, waits for them, and re-layouts, body(): lax.map(per_head, (query_blocks, key_window, value_window))  11.5 us
    dot_general x12, matrix products, attend_rows(): jnp.einsum('rtmu,rmud->rtd', grad_scores_b, key_tiles, preferred_element_...  11.3 us
  transfers between devices with their start and end apart: 10, of which 6 were waited for; matrix products, arithmetic and copies ran while one was open for 9% of the time, Pallas kernels for 0%

commit v1 on v0

v1 whole, which is shorter than its diff:
```python
import functools

import jax
import jax.numpy as jnp
from jax import lax
from jax.experimental import pallas as pl
from jax.experimental.pallas import tpu as pltpu
from jax.sharding import PartitionSpec as P

HD = 128
BLK = 128
CHB = 2
TEAM = 8
MESH = pl.DeviceIdType.MESH

loss_scale = 64.0
masked = -1e30
log2e = 1.4426950408889634


def dot(a, b, da, db):
    return lax.dot_general(a, b, (((da,), (db,)), ((), ())), preferred_element_type=jnp.float32)


def kernel(
    cfg,
    q_hbm, k_hbm, v_hbm, mask_ref,
    dq_hbm, dk_hbm, dv_hbm,
    qbuf, kbuf, vbuf, bbuf, bias_own, acc_k, acc_v,
    dq_st, dk_st, dv_st, gsend, grecv,
    f_send, f_recv, f_own, b_send, b_recv, m_sem,
    h_send, h_recv, r_send, r_recv, o_send, o_recv, o_own,
):
    span, ulys, teams, nh, halo, nb = cfg
    team = span * ulys
    rows = team * BLK
    hb = halo // BLK
    ch = CHB * BLK
    win = 2 * halo + ch
    wb = win // BLK
    nchunks = rows // ch
    scale = HD ** (-0.5)

    blk = lax.axis_index("blk")
    uly = lax.axis_index("uly")
    group = blk // span
    me = (blk % span) * ulys + uly
    has_lower = group > 0
    has_upper = group < teams - 1

    def device(index):
        return (group * span + index // ulys, index % ulys)

    lower = (blk - span, uly)
    upper = (blk + span, uly)

    barrier = pltpu.get_barrier_semaphore()

    def hello(d, _):
        pl.semaphore_signal(
            barrier, inc=1, device_id=device((me + d) % team), device_id_type=MESH
        )
        return 0

    lax.fori_loop(1, team, hello, 0)

    @pl.when(has_lower)
    def _():
        pl.semaphore_signal(barrier, inc=1, device_id=lower, device_id_type=MESH)

    @pl.when(has_upper)
    def _():
        pl.semaphore_signal(barrier, inc=1, device_id=upper, device_id_type=MESH)

    wpad = bias_own.shape[0]
    row_of = lax.broadcasted_iota(jnp.int32, mask_ref.shape, 0)
    own_row = jnp.sum(
        jnp.where(row_of == uly, mask_ref[...], 0).astype(jnp.float32), axis=0, keepdims=True
    )
    start = (group * team + (me // CHB) * CHB) - hb
    col = lax.broadcasted_iota(jnp.int32, (wpad, nb), 1)
    want = lax.broadcasted_iota(jnp.int32, (wpad, nb), 0) + start
    allowed = jnp.sum(
        jnp.where(col == want, jnp.broadcast_to(own_row, (wpad, nb)), 0.0), axis=1, keepdims=True
    )
    bias_own[...] = jnp.broadcast_to((1.0 - allowed) * masked, (wpad, BLK))

    beside = has_lower.astype(jnp.int32) + has_upper.astype(jnp.int32)
    pl.semaphore_wait(barrier, team - 1 + beside)

    my_rows = pl.multiple_of(me * BLK, BLK)

    def columns(owner, j):
        return pl.ds(pl.multiple_of((owner * nh + j) * HD, HD), HD)

    inputs = ((q_hbm, qbuf, 0), (k_hbm, kbuf, halo), (v_hbm, vbuf, halo))

    def push_mask(d, _):
        pltpu.make_async_remote_copy(
            src_ref=bias_own, dst_ref=bbuf.at[me], send_sem=b_send, recv_sem=b_recv,
            device_id=device((me + d) % team), device_id_type=MESH,
        ).start()
        return 0

    lax.fori_loop(1, team, push_mask, 0)

    def push_head(j, _):
        for a, (src, dst, offset) in enumerate(inputs):
            pltpu.make_async_copy(
                src.at[:, columns(me, j)],
                dst.at[j, pl.ds(my_rows + offset, BLK), :],
                f_own.at[a, j],
            ).start()

        def push_peer(d, _):
            peer = (me + d) % team
            for a, (src, dst, offset) in enumerate(inputs):
                pltpu.make_async_remote_copy(
                    src_ref=src.at[:, columns(peer, j)],
                    dst_ref=dst.at[j, pl.ds(my_rows + offset, BLK), :],
                    send_sem=f_send.at[a, j], recv_sem=f_recv.at[a, j],
                    device_id=device(peer), device_id_type=MESH,
                ).start()
            return 0

        lax.fori_loop(1, team, push_peer, 0)
        return 0

    lax.fori_loop(0, nh, push_head, 0)

    own_bias = pltpu.make_async_copy(bias_own, bbuf.at[me], m_sem)
    own_bias.start()
    own_bias.wait()

    acc_k[...] = jnp.zeros_like(acc_k)
    acc_v[...] = jnp.zeros_like(acc_v)
    edge = jnp.zeros((nh, halo, HD), jnp.bfloat16)

    @pl.when(jnp.logical_not(has_lower))
    def _():
        kbuf[:, 0:halo, :] = edge
        vbuf[:, 0:halo, :] = edge

    @pl.when(jnp.logical_not(has_upper))
    def _():
        kbuf[:, halo + rows :, :] = edge
        vbuf[:, halo + rows :, :] = edge

    def drain(ref, sem):
        pltpu.make_async_copy(ref, ref, sem).wait()

    peers_rows = (team - 1) * BLK
    drain(bbuf.at[pl.ds(0, team - 1)], b_recv)

    def halo_copies(j, side):
        place = halo if side == 0 else rows
        land = halo + rows if side == 0 else 0
        return [
            pltpu.make_async_remote_copy(
                src_ref=buf.at[j, pl.ds(place, halo), :],
                dst_ref=buf.at[j, pl.ds(land, halo), :],
                send_sem=h_send.at[a, j, side], recv_sem=h_recv.at[a, j, side],
                device_id=lower if side == 0 else upper, device_id_type=MESH,
            )
            for a, buf in enumerate((kbuf, vbuf))
        ]

    def grad_copies(j, side):
        return [
            pltpu.make_async_remote_copy(
                src_ref=gsend.at[a, j, side], dst_ref=grecv.at[a, j, side],
                send_sem=r_send.at[a, j, side], recv_sem=r_recv.at[a, j, side],
                device_id=lower if side == 0 else upper, device_id_type=MESH,
            )
            for a in range(2)
        ]

    there = (has_lower, has_upper)

    def send_block(a, j, block):
        st, out = ((dq_st, dq_hbm), (dk_st, dk_hbm), (dv_st, dv_hbm))[a]
        src = st.at[j, pl.ds(block * BLK, BLK), :]
        dst = out.at[:, columns(me, j)]

        @pl.when(me == block)
        def _():
            pltpu.make_async_copy(src, dst, o_own.at[a, j]).start()

        @pl.when(me != block)
        def _():
            pltpu.make_async_remote_copy(
                src_ref=src, dst_ref=dst, send_sem=o_send.at[a, j], recv_sem=o_recv.at[a, j],
                device_id=device(block), device_id_type=MESH,
            ).start()

    def chunk(j, c):
        base = c * ch
        k = kbuf[j, base : base + win, :]
        v = vbuf[j, base : base + win, :]
        q = qbuf[j, base : base + ch, :]
        bias = jnp.concatenate([bbuf[c * CHB + i] for i in range(CHB)], axis=1)[:wb]
        s = dot(k, q, 1, 1).reshape(wb, BLK, ch) * (scale * log2e) + bias[:, None, :]
        top = jnp.max(jnp.max(s, axis=0), axis=0, keepdims=True)
        p = jnp.exp2(s - top[None])
        total = jnp.sum(jnp.sum(p, axis=0), axis=0, keepdims=True)
        p = p.reshape(win, ch)
        pb = p.astype(jnp.bfloat16)
        inv = 1.0 / total
        o = dot(v, pb, 0, 0) * inv
        g = (loss_scale * o * inv).astype(jnp.bfloat16)
        delta = jnp.sum(g.astype(jnp.float32) * o, axis=0, keepdims=True)
        acc_v[j, base : base + win, :] += dot(pb, g, 1, 1)
        ds = (p * (dot(v, g, 1, 0) - delta)).astype(jnp.bfloat16)
        acc_k[j, base : base + win, :] += dot(ds, q, 1, 0)
        dq = dot(k, ds, 0, 0) * scale
        dq_st[j, base : base + ch, :] = dq.T.astype(jnp.bfloat16)
        for i in range(CHB):
            send_block(0, j, c * CHB + i)

    def finish_block(j, block):
        at = halo + block * BLK
        here = slice(block * BLK, (block + 1) * BLK)
        dk_st[j, here, :] = (acc_k[j, at : at + BLK, :] * scale).astype(jnp.bfloat16)
        dv_st[j, here, :] = acc_v[j, at : at + BLK, :].astype(jnp.bfloat16)
        send_block(1, j, block)
        send_block(2, j, block)

    inner_blocks = [b for b in range(team) if hb <= b < team - hb]
    outer_blocks = [b for b in range(team) if b not in inner_blocks]
    inner_chunks = [c for c in range(nchunks) if c * ch >= halo and c * ch + ch + halo <= rows]
    outer_chunks = [c for c in range(nchunks) if c not in inner_chunks]

    def finish_outer(j):
        for side in range(2):
            @pl.when(there[1 - side])
            def _():
                for copy in grad_copies(j, side):
                    copy.wait_recv()
                at = halo if side == 1 else rows
                acc_k[j, at : at + halo, :] += grecv[0, j, side].astype(jnp.float32)
                acc_v[j, at : at + halo, :] += grecv[1, j, side].astype(jnp.float32)

        for block in outer_blocks:
            finish_block(j, block)

    def head(j, _):
        for a, (src, dst, offset) in enumerate(inputs):
            drain(dst.at[j, pl.ds(offset, peers_rows), :], f_recv.at[a, j])
            drain(dst.at[j, pl.ds(offset, BLK), :], f_own.at[a, j])
        for side in range(2):
            @pl.when(there[side])
            def _():
                for copy in halo_copies(j, side):
                    copy.start()

        for c in inner_chunks:
            chunk(j, c)

        @pl.when(j > 0)
        def _():
            finish_outer(j - 1)

        for side in range(2):
            @pl.when(there[1 - side])
            def _():
                for copy in halo_copies(j, side):
                    copy.wait_recv()

        for c in outer_chunks:
            chunk(j, c)

        for side in range(2):
            @pl.when(there[side])
            def _():
                at = 0 if side == 0 else halo + rows
                gsend[0, j, side] = acc_k[j, at : at + halo, :].astype(jnp.bfloat16)
                gsend[1, j, side] = acc_v[j, at : at + halo, :].astype(jnp.bfloat16)
                for copy in grad_copies(j, side):
                    copy.start()

        for block in inner_blocks:
            finish_block(j, block)
        return 0

    lax.fori_loop(0, nh, head, 0)
    finish_outer(nh - 1)

    drain(bbuf.at[pl.ds(0, team - 1)], b_send)

    def settle(j, _):
        for a, (src, dst, offset) in enumerate(inputs):
            drain(dst.at[j, pl.ds(offset, peers_rows), :], f_send.at[a, j])
        for side in range(2):
            @pl.when(there[side])
            def _():
                for copy in halo_copies(j, side) + grad_copies(j, side):
                    copy.wait_send()

        for a, st in enumerate((dq_st, dk_st, dv_st)):
            drain(st.at[j, pl.ds(0, peers_rows), :], o_send.at[a, j])
            drain(st.at[j, pl.ds(0, BLK), :], o_own.at[a, j])
            drain(st.at[j, pl.ds(0, peers_rows), :], o_recv.at[a, j])
        return 0

    lax.fori_loop(0, nh, settle, 0)


def body(query, keys, values, block_mask):
    blks = lax.axis_size("blk")
    ulys = lax.axis_size("uly")
    heads_all = query.shape[1] // HD
    span = max(1, TEAM // ulys)
    team = span * ulys
    nh = heads_all // team
    halo = query.shape[0] * ulys
    rows = team * BLK
    nb = block_mask.shape[1]
    cfg = (span, ulys, blks // span, nh, halo, nb)
    wpad = -(-(2 * halo // BLK + CHB) // 8) * 8
    bf, f32 = jnp.bfloat16, jnp.float32
    dma = pltpu.SemaphoreType.DMA
    anywhere = pl.BlockSpec(memory_space=pl.ANY)
    return pl.pallas_call(
        functools.partial(kernel, cfg),
        out_shape=[jax.ShapeDtypeStruct(query.shape, bf)] * 3,
        in_specs=[anywhere] * 3 + [pl.BlockSpec(memory_space=pltpu.VMEM)],
        out_specs=[anywhere] * 3,
        scratch_shapes=[
            pltpu.VMEM((nh, rows, HD), bf),
            pltpu.VMEM((nh, rows + 2 * halo, HD), bf),
            pltpu.VMEM((nh, rows + 2 * halo, HD), bf),
            pltpu.VMEM((team, wpad, BLK), f32),
            pltpu.VMEM((wpad, BLK), f32),
            pltpu.VMEM((nh, rows + 2 * halo, HD), f32),
            pltpu.VMEM((nh, rows + 2 * halo, HD), f32),
            pltpu.VMEM((nh, rows, HD), bf),
            pltpu.VMEM((nh, rows, HD), bf),
            pltpu.VMEM((nh, rows, HD), bf),
            pltpu.VMEM((2, nh, 2, halo, HD), bf),
            pltpu.VMEM((2, nh, 2, halo, HD), bf),
            dma((3, nh)), dma((3, nh)), dma((3, nh)),
            dma, dma, dma,
            dma((2, nh, 2)), dma((2, nh, 2)), dma((2, nh, 2)), dma((2, nh, 2)),
            dma((3, nh)), dma((3, nh)), dma((3, nh)),
        ],
        compiler_params=pltpu.CompilerParams(
            collective_id=0, has_side_effects=True, vmem_limit_bytes=56 * 1024 * 1024
        ),
    )(query, keys, values, block_mask)


def solution(mesh):
    in_specs = (
        P(("blk", "uly"), None),
        P(("blk", "uly"), None),
        P(("blk", "uly"), None),
        P("blk", None),
    )
    out_specs = (P(("blk", "uly"), None), P(("blk", "uly"), None), P(("blk", "uly"), None))
    return jax.shard_map(body, mesh=mesh, in_specs=in_specs, out_specs=out_specs, check_vma=False)
```

time: 273 us -> 63.5 us (0.23)
  the two profiles are of different devices: /device:TPU:9 before, /device:TPU:0 now
where the time goes in v1:
time: 63.5 us; the launch traced here: 63.3 us
  Pallas kernels  58.2 us (92%)
  local copies, waits for them, and re-layouts  4.44 us (7%)
  between operations  0.65 us (1%)
    pallas_call x1, Pallas kernels, body(): pl.pallas_call(functools.partial(kernel, cfg), out_shape=[jax.ShapeDtypeS...  58.2 us
    unnamed x7, local copies, waits for them, and re-layouts  4.44 us

profile of v1, /device:TPU:0, one launch (start us, length us, event | category | flops | bytes accessed | tf_op | source)
XLA Modules:
  0.0 63.3 jit_solution(993281662281489050)
XLA Ops:
  0.6 58.2 %shard_map.67 = (bf16[128,3072]{1,0:T(8,128)(2,1)}, bf16[128,3072]{1,0:T(8,128)(2,1)}, bf16[128,3072]{1,0:T(8,128)(2,1)}) custom-call(bf16[128,3072]{1,0:T(8,128)(2,1)} %q_hbm.1, bf16[128,3072]{1,0:T(8,128)(2,1)} %k_hbm.1, bf16[128,3072]{1,0:T(8,128)(2,1)} %v_hbm.1, s32[2,32]{1,0:T(2,128)} %mask_ref.1), custom_call_target="tpu_custom_call" | custom-call | tf_op jit(solution)/shard_map/pallas_call | solution.py:323
  58.8 0.0 copy-start.1
  58.9 2.1 %copy.10 = bf16[128,3072]{1,0:T(8,128)(2,1)} copy(bf16[128,3072]{1,0:T(8,128)(2,1)} %get-tuple-element.6) | data formatting | bytes 1572864
  61.0 0.0 copy-done.1
  61.0 0.0 copy-start
  61.0 0.9 %copy.11 = bf16[128,3072]{1,0:T(8,128)(2,1)} copy(bf16[128,3072]{1,0:T(8,128)(2,1)S(1)} %copy-done.1) | data formatting | bytes 1572864
  61.9 0.5 copy-done
  62.4 0.9 %copy.12 = bf16[128,3072]{1,0:T(8,128)(2,1)} copy(bf16[128,3072]{1,0:T(8,128)(2,1)S(1)} %copy-done) | data formatting | bytes 1572864
Async XLA Ops:
  58.8 2.1 %copy-start.1 = (bf16[128,3072]{1,0:T(8,128)(2,1)S(1)}, bf16[128,3072]{1,0:T(8,128)(2,1)}, u32[]{:S(2)}) copy-start(bf16[128,3072]{1,0:T(8,128)(2,1)} %get-tuple-element.7) | copy-start | bytes 2359300
  61.0 1.4 %copy-start = (bf16[128,3072]{1,0:T(8,128)(2,1)S(1)}, bf16[128,3072]{1,0:T(8,128)(2,1)}, u32[]{:S(2)}) copy-start(bf16[128,3072]{1,0:T(8,128)(2,1)} %get-tuple-element.8) | copy-start | bytes 2359300

commit v2 on v1

--- a/solution.py
+++ b/solution.py
@@ -10,6 +10,7 @@
 HD = 128
 BLK = 128
 CHB = 2
+PIECES = 4
 TEAM = 8
 MESH = pl.DeviceIdType.MESH
 
@@ -305,6 +306,33 @@
     lax.fori_loop(0, nh, settle, 0)
 
 
+def write_out(*refs):
+    n = len(refs) // 2
+    srcs, dsts, sem = refs[: n], refs[n : 2 * n], refs[2 * n]
+    copies = []
+    for a, (src, dst) in enumerate(zip(srcs, dsts)):
+        step = src.shape[0] // PIECES
+        for i in range(PIECES):
+            here = pl.ds(i * step, step)
+            copies.append(pltpu.make_async_copy(src.at[here], dst.at[here], sem.at[a, i]))
+    for copy in copies:
+        copy.start()
+    for copy in copies:
+        copy.wait()
+
+
+def written(*arrays):
+    anywhere = pl.BlockSpec(memory_space=pl.ANY)
+    return pl.pallas_call(
+        write_out,
+        out_shape=[jax.ShapeDtypeStruct(a.shape, a.dtype) for a in arrays],
+        in_specs=[anywhere] * len(arrays),
+        out_specs=[pl.BlockSpec(memory_space=pltpu.HBM)] * len(arrays),
+        scratch_shapes=[pltpu.SemaphoreType.DMA((len(arrays), PIECES))],
+        compiler_params=pltpu.CompilerParams(vmem_limit_bytes=2 * 1024 * 1024),
+    )(*arrays)
+
+
 def body(query, keys, values, block_mask):
     blks = lax.axis_size("blk")
     ulys = lax.axis_size("uly")
@@ -317,13 +345,14 @@
     nb = block_mask.shape[1]
     cfg = (span, ulys, blks // span, nh, halo, nb)
     wpad = -(-(2 * halo // BLK + CHB) // 8) * 8
+    grant = 51 if halo <= 2 * BLK else 56
     bf, f32 = jnp.bfloat16, jnp.float32
     dma = pltpu.SemaphoreType.DMA
     anywhere = pl.BlockSpec(memory_space=pl.ANY)
-    return pl.pallas_call(
+    grads = pl.pallas_call(
         functools.partial(kernel, cfg),
         out_shape=[jax.ShapeDtypeStruct(query.shape, bf)] * 3,
-        in_specs=[anywhere] * 3 + [pl.BlockSpec(memory_space=pltpu.VMEM)],
+        in_specs=[pl.BlockSpec(memory_space=pltpu.HBM)] * 3 + [pl.BlockSpec(memory_space=pltpu.VMEM)],
         out_specs=[anywhere] * 3,
         scratch_shapes=[
             pltpu.VMEM((nh, rows, HD), bf),
@@ -344,9 +373,10 @@
             dma((3, nh)), dma((3, nh)), dma((3, nh)),
         ],
         compiler_params=pltpu.CompilerParams(
-            collective_id=0, has_side_effects=True, vmem_limit_bytes=56 * 1024 * 1024
+            collective_id=0, has_side_effects=True, vmem_limit_bytes=grant * 1024 * 1024
         ),
     )(query, keys, values, block_mask)
+    return written(*grads)
 
 
 def solution(mesh):

time: 63.5 us -> 60.4 us (0.951)
  local copies, waits for them, and re-layouts: 4.44 us -> 0.67 us
  Pallas kernels: 58.2 us -> 58.9 us
    unnamed x7 -> x2, local copies, waits for them, and re-layouts: 4.44 us -> 0.67 us
    pallas_call x0 -> x1, Pallas kernels: none -> 1.49 us  [written(): pl.pallas_call(write_out, out_shape=[jax.ShapeDtypeStruct(a.shape, a.dtyp...]
    pallas_call x1, Pallas kernels: 58.2 us -> 57.4 us  [body(): pl.pallas_call(functools.partial(kernel, cfg), out_shape=[jax.ShapeDtypeS...]
where the time goes in v2:
time: 60.4 us; the launch traced here: 60.2 us
  Pallas kernels  58.9 us (98%)
  local copies, waits for them, and re-layouts  0.67 us (1%)
  between operations  0.65 us (1%)
    pallas_call x1, Pallas kernels, body(): pl.pallas_call(functools.partial(kernel, cfg), out_shape=[jax.ShapeDtypeS...  57.4 us
    pallas_call x1, Pallas kernels, written(): pl.pallas_call(write_out, out_shape=[jax.ShapeDtypeStruct(a.shape, a.dtyp...  1.49 us

profile of v2, /device:TPU:0, one launch (start us, length us, event | category | flops | bytes accessed | tf_op | source)
XLA Modules:
  0.0 60.2 jit_solution(12557174003937650370)
XLA Ops:
  0.6 0.0 copy-start
  0.6 0.7 %copy-done = s32[2,32]{1,0:T(2,128)S(1)} copy-done((s32[2,32]{1,0:T(2,128)S(1)}, s32[2,32]{1,0:T(2,128)}, u32[]{:S(2)}) %copy-start) | copy-done | bytes 280
  1.3 57.4 %shard_map.67 = (bf16[128,3072]{1,0:T(8,128)(2,1)S(1)}, bf16[128,3072]{1,0:T(8,128)(2,1)S(1)}, bf16[128,3072]{1,0:T(8,128)(2,1)S(1)}) custom-call(bf16[128,3072]{1,0:T(8,128)(2,1)} %q_hbm.1, bf16[128,3072]{1,0:T(8,128)(2,1)} %k_hbm.1, bf16[128,3072]{1,0:T(8,128)(2,1)} %v_hbm.1, s32[2,32]{1,0:T(2,128)S(1)} %copy-done), custom_call_target="tpu_custom_call" | custom-call | tf_op jit(solution)/shard_map/pallas_call | solution.py:352
  58.7 1.5 %shard_map.68 = (bf16[128,3072]{1,0:T(8,128)(2,1)}, bf16[128,3072]{1,0:T(8,128)(2,1)}, bf16[128,3072]{1,0:T(8,128)(2,1)}) custom-call(bf16[128,3072]{1,0:T(8,128)(2,1)S(1)} %get-tuple-element.6.refs_0_, bf16[128,3072]{1,0:T(8,128)(2,1)S(1)} %get-tuple-element.7.refs_1_, bf16[128,3072]{1,0:T(8,128)(2,1)S(1)} %get-tuple-element.8.refs_2_), custom_call_target="tpu_custom_call" | custom-call | tf_op jit(solution)/shard_map/pallas_call | solution.py:326
Async XLA Ops:
  0.6 0.7 %copy-start = (s32[2,32]{1,0:T(2,128)S(1)}, s32[2,32]{1,0:T(2,128)}, u32[]{:S(2)}) copy-start(s32[2,32]{1,0:T(2,128)} %mask_ref.1) | copy-start | bytes 772
